TPU v7x, 128 devices: a whole 4x4x4 slice. The times are simulated.
128 devices in a mesh: dp: 16 (over y, z_hi, core), row: 4 (over x), col: 2 (over z_lo).
Axes of the slice: x: 4, y: 4, z: 4 (z_hi: 2, z_lo: 2; z = z_hi * 2 + z_lo), core: 2. Of those that a mesh axis runs over, the one named last changes fastest.
Arguments:
- inputs: bfloat16 [16, 1024, 1152], P('dp', 'row', 'col'), may hold values from -6 to 6
- w_query: bfloat16 [1152, 1024], P('col', 'row'), may hold values from -0.1875 to 0.1875
- w_key: bfloat16 [1152, 256], P('col'), may hold values from -0.1875 to 0.1875
- w_value: bfloat16 [1152, 256], P('col'), may hold values from -0.1875 to 0.1875
- attention_output_weight: bfloat16 [1024, 1152], P('row', 'col'), may hold values from -0.1875 to 0.1875
- w_gate: bfloat16 [1152, 6912], P('col', 'row'), may hold values from -0.1875 to 0.1875
- w_up: bfloat16 [1152, 6912], P('col', 'row'), may hold values from -0.1875 to 0.1875
- down_weight: bfloat16 [6912, 1152], P('row', 'col'), may hold values from -0.078125 to 0.078125
- g_in: float32 [1152], P('col'), may hold values from 0.25 to 1.75
- g_query: float32 [256], replicated, may hold values from 0.25 to 1.75
- g_key: float32 [256], replicated, may hold values from 0.25 to 1.75
- g_post_attn: float32 [1152], P('col'), may hold values from 0.25 to 1.75
- g_pre_ffn: float32 [1152], P('col'), may hold values from 0.25 to 1.75
- g_post_ffn: float32 [1152], P('col'), may hold values from 0.25 to 1.75
- cotangent: bfloat16 [16, 1024, 1152], P('dp', 'row', 'col'), may hold values from -6 to 6
Outputs:
- block_out: bfloat16 [16, 1024, 1152], P('dp', 'row', 'col')
- grad_inputs: bfloat16 [16, 1024, 1152], P('dp', 'row', 'col')
- grad_w_query: float32 [1152, 1024], P('col', 'row')
- grad_w_key: float32 [1152, 256], P('col')
- grad_w_value: float32 [1152, 256], P('col')
- grad_w_out: float32 [1024, 1152], P('row', 'col')
- grad_w_gate: float32 [1152, 6912], P('col', 'row')
- grad_w_up: float32 [1152, 6912], P('col', 'row')
- grad_w_down: float32 [6912, 1152], P('row', 'col')
- grad_g_in: float32 [1152], P('col')
- grad_g_query: float32 [256], replicated
- grad_g_key: float32 [256], replicated
- grad_g_post_attn: float32 [1152], P('col')
- grad_g_pre_ffn: float32 [1152], P('col')
- grad_g_post_ffn: float32 [1152], P('col')
All inputs are finite; a program needn't handle non-finite values.
Results may differ from a plain program's by a relative error of at most 0.025.
Values may be sent and summed in bfloat16 or wider, within the bound.
No kernel may reach another device: no remote copies, remote signals or barrier semaphores. Data moves between devices by JAX's collectives and lax.ppermute only.
A program may use at most 128 MiB of HBM per device.

v0:
```python
from functools import partial
import jax
import jax.numpy as jnp
from jax import lax
from jax.sharding import PartitionSpec as P

WINDOW = 512
EPSILON = 1e-06
MASKED = -1e30
ROPE_BASE = 10000.0


def sent_to_all(shard, axis):
    copies = jnp.broadcast_to(shard, (lax.axis_size(axis), *shard.shape))
    return lax.all_to_all(copies, axis, split_axis=0, concat_axis=0, tiled=True)


def of_everyone(shard, axis):
    return sent_to_all(shard, axis).sum(axis=0)


def laid_out(parts, dim):
    shape = list(parts.shape[1:])
    shape[dim] *= parts.shape[0]
    return jnp.moveaxis(parts, 0, dim).reshape(shape)


def gather_directly(shard, axis, dim):
    return laid_out(sent_to_all(shard, axis), dim)


def cut_along(shard, dim, length):
    before, after = (shard.shape[:dim], shard.shape[dim + 1 :])
    return jnp.moveaxis(shard.reshape(*before, length, -1, *after), dim, 0)


def summed_on_arrival(shard, axis, dim):
    length = lax.axis_size(axis)
    parts = lax.all_to_all(cut_along(shard, dim, length), axis, 0, 0, tiled=True)
    return jnp.sum(parts.astype(jnp.float32), axis=0)


def passed_along(block, axis, distance):
    devices = range(lax.axis_size(axis))
    route = [(i - distance, i) for i in devices if i - distance in devices]
    return lax.ppermute(block, axis, route)


def feature_sums(partial_sum):
    return of_everyone(partial_sum, "col")


def row_gather(values):
    return gather_directly(values, "row", 1)


def col_gather(values):
    return lax.all_gather(values, "col", axis=1, tiled=True)


def row_sums(values):
    return summed_on_arrival(values.astype(jnp.bfloat16), "row", 1)


def reduce_feature_axis(full_rows, weight_whole, pattern):
    whole_rows = lax.all_to_all(full_rows, "col", split_axis=1, concat_axis=2, tiled=True)
    return jnp.einsum(pattern, whole_rows, weight_whole, preferred_element_type=jnp.float32)


def norm_forward(values, gain_vec, feature_count):
    squares = feature_sums(jnp.sum(values * values, axis=-1, keepdims=True))
    factor = lax.rsqrt(squares / feature_count + EPSILON)
    return (values * factor * gain_vec, factor)


def norm_backward(values, factor, gain_vec, upstream, feature_count):
    scaled = upstream * gain_vec
    inner = feature_sums(jnp.sum(scaled * values, axis=-1, keepdims=True))
    grad_values = factor * scaled - values * (factor * factor * factor) * inner / feature_count
    grad_gain = jnp.sum(upstream * values * factor, axis=(0, 1))
    return (grad_values, grad_gain)


def rotate(values, position):
    half_size = values.shape[-1] // 2
    exponent = jnp.arange(half_size, dtype=jnp.float32) * (2.0 / values.shape[-1])
    angles = position.astype(jnp.float32)[:, None] * (ROPE_BASE ** (-exponent))[None, :]
    cosine = jnp.cos(angles)
    sine = jnp.sin(angles)
    first = values[..., :half_size]
    second = values[..., half_size:]
    return jnp.concatenate(
        [first * cosine - second * sine, second * cosine + first * sine], axis=-1
    )


def head_map(raw_heads, gain_vec, position, scaling):
    normed = (
        raw_heads
        * lax.rsqrt(jnp.mean(raw_heads * raw_heads, axis=-1, keepdims=True) + EPSILON)
        * gain_vec
    )
    return rotate(normed, position) * scaling


def geglu(gate_proj, up_proj):
    return jax.nn.gelu(gate_proj, approximate=True) * up_proj


def local(
    inputs,
    w_query,
    w_key,
    w_value,
    attention_output_weight,
    w_gate,
    w_up,
    down_weight,
    g_in,
    g_query,
    g_key,
    g_post_attn,
    g_pre_ffn,
    g_post_ffn,
    cotangent,
):
    col_count = lax.axis_size("col")
    col_index = lax.axis_index("col")
    seq_count, row_share, feature_share = inputs.shape
    feature_count = feature_share * col_count
    head_size = g_query.shape[0]
    heads_local = w_query.shape[1] // head_size
    query_width = heads_local * head_size
    hidden_share = w_gate.shape[1]
    length = row_share * lax.axis_size("row")
    half_rows = length // col_count
    position = col_index * half_rows + jnp.arange(half_rows, dtype=jnp.int32)
    key_position = (col_index - 1) * half_rows + jnp.arange(2 * half_rows, dtype=jnp.int32)
    offset = position[:, None] - key_position[None, :]
    allowed = (offset >= 0) & (offset < WINDOW) & (key_position[None, :] >= 0)
    query_key_value_weight = jnp.concatenate([w_query, w_key, w_value], axis=1)
    paired_weight = jnp.concatenate([w_gate, w_up], axis=1)
    qkv_whole, pair_whole, out_whole, down_whole = (
        lax.all_gather(query_key_value_weight, "col", axis=0, tiled=True),
        lax.all_gather(paired_weight, "col", axis=0, tiled=True),
        lax.all_gather(attention_output_weight, "col", axis=1, tiled=True),
        lax.all_gather(down_weight, "col", axis=1, tiled=True),
    )
    inputs_wide = inputs.astype(jnp.float32)
    attn_norm, attn_factor = norm_forward(inputs_wide, g_in, feature_count)
    attention_complete = row_gather(attn_norm.astype(jnp.bfloat16))
    query_key_value_total = reduce_feature_axis(attention_complete, qkv_whole, "rit,th->rih")
    raw_query = (
        query_key_value_total[..., :query_width]
        .reshape(seq_count, half_rows, heads_local, head_size)
        .transpose(0, 2, 1, 3)
    )
    raw_key = query_key_value_total[:, None, :, query_width : query_width + head_size]
    value_low = query_key_value_total[..., query_width + head_size :].astype(jnp.bfloat16)
    query_rot, query_pull = jax.vjp(
        partial(head_map, position=position, scaling=head_size ** (-0.5)), raw_query, g_query
    )
    key_rot, key_pull = jax.vjp(partial(head_map, position=position, scaling=1.0), raw_key, g_key)
    query_low = query_rot.astype(jnp.bfloat16)
    key_low = key_rot[:, 0].astype(jnp.bfloat16)
    key_prev, value_prev = passed_along((key_low, value_low), "col", 1)
    key_all = jnp.concatenate([key_prev, key_low], axis=1)
    value_all = jnp.concatenate([value_prev, value_low], axis=1)
    scores = jnp.where(
        allowed,
        jnp.einsum("shqd,skd->shqk", query_low, key_all, preferred_element_type=jnp.float32),
        MASKED,
    )
    largest = jnp.max(scores, axis=-1, keepdims=True)
    summed = jnp.sum(jnp.exp(scores - largest), axis=-1, keepdims=True)
    log_total = largest + jnp.log(summed)
    attn_probs = jnp.exp(scores - log_total)
    mixed_heads = jnp.einsum(
        "shqk,skd->shqd",
        attn_probs.astype(jnp.bfloat16),
        value_all,
        preferred_element_type=jnp.float32,
    )
    mixed_low = (
        mixed_heads.astype(jnp.bfloat16)
        .transpose(0, 2, 1, 3)
        .reshape(seq_count, half_rows, query_width)
    )
    mixed_complete = col_gather(mixed_low)
    branch = row_sums(
        jnp.einsum(
            "cfb,bi->cfi",
            mixed_complete,
            attention_output_weight,
            preferred_element_type=jnp.float32,
        )
    )
    post_attn, post_factor = norm_forward(branch, g_post_attn, feature_count)
    middle = inputs_wide + post_attn
    ffn_norm, ffn_factor = norm_forward(middle, g_pre_ffn, feature_count)
    feedforward_complete = row_gather(ffn_norm.astype(jnp.bfloat16))
    paired_partial_total = reduce_feature_axis(feedforward_complete, pair_whole, "nax,xu->nau")
    hidden, geglu_pull = jax.vjp(
        geglu, paired_partial_total[..., :hidden_share], paired_partial_total[..., hidden_share:]
    )
    hidden_complete = col_gather(hidden.astype(jnp.bfloat16))
    down_proj = row_sums(
        jnp.einsum("yat,tn->yan", hidden_complete, down_weight, preferred_element_type=jnp.float32)
    )
    post_ffn, post_ffn_factor = norm_forward(down_proj, g_post_ffn, feature_count)
    block_out = (middle + post_ffn).astype(jnp.bfloat16)
    upstream = cotangent.astype(jnp.float32)
    grad_down, grad_g_post_ffn = norm_backward(
        down_proj, post_ffn_factor, g_post_ffn, upstream, feature_count
    )
    down_gradient_complete = row_gather(grad_down.astype(jnp.bfloat16))
    grad_w_down = jnp.einsum(
        "hwk,hwj->kj", hidden_complete, down_gradient_complete, preferred_element_type=jnp.float32
    )
    hidden_gradient = reduce_feature_axis(down_gradient_complete, down_whole, "qrn,on->qro")
    grad_gate, grad_up = geglu_pull(hidden_gradient)
    grad_pair = jnp.concatenate(
        [grad_gate.astype(jnp.bfloat16), grad_up.astype(jnp.bfloat16)], axis=-1
    )
    paired_gradient_complete = col_gather(grad_pair)
    grad_w_pair = jnp.einsum(
        "wkb,wkg->bg",
        feedforward_complete,
        paired_gradient_complete,
        preferred_element_type=jnp.float32,
    )
    grad_w_gate = grad_w_pair[:, :hidden_share]
    grad_w_up = grad_w_pair[:, hidden_share:]
    grad_ffn_in = row_sums(
        jnp.einsum(
            "bvq,eq->bve",
            paired_gradient_complete,
            paired_weight,
            preferred_element_type=jnp.float32,
        )
    )
    grad_mid_norm, grad_g_pre_ffn = norm_backward(
        middle, ffn_factor, g_pre_ffn, grad_ffn_in, feature_count
    )
    grad_middle = upstream + grad_mid_norm
    grad_branch, grad_g_post_attn = norm_backward(
        branch, post_factor, g_post_attn, grad_middle, feature_count
    )
    branch_gradient_complete = row_gather(grad_branch.astype(jnp.bfloat16))
    grad_w_out = jnp.einsum(
        "jyh,jyp->hp", mixed_complete, branch_gradient_complete, preferred_element_type=jnp.float32
    )
    mixed_gradient = reduce_feature_axis(branch_gradient_complete, out_whole, "afm,rm->afr")
    grad_mixed_low = (
        mixed_gradient.astype(jnp.bfloat16)
        .reshape(seq_count, half_rows, heads_local, head_size)
        .transpose(0, 2, 1, 3)
    )
    scores_again = jnp.where(
        allowed,
        jnp.einsum("shqd,skd->shqk", query_low, key_all, preferred_element_type=jnp.float32),
        MASKED,
    )
    probs_again = jnp.exp(scores_again - log_total)
    grad_probs = jnp.einsum(
        "shqd,skd->shqk", grad_mixed_low, value_all, preferred_element_type=jnp.float32
    )
    grad_value_all = jnp.einsum(
        "shqk,shqd->shkd",
        probs_again.astype(jnp.bfloat16),
        grad_mixed_low,
        preferred_element_type=jnp.float32,
    )
    grad_scores = (
        probs_again * (grad_probs - jnp.sum(probs_again * grad_probs, axis=-1, keepdims=True))
    ).astype(jnp.bfloat16)
    grad_query_rot = jnp.einsum(
        "shqk,skd->shqd", grad_scores, key_all, preferred_element_type=jnp.float32
    )
    grad_key_all = jnp.einsum(
        "shqk,shqd->shkd", grad_scores, query_low, preferred_element_type=jnp.float32
    )
    key_back, value_back = (
        passed_along(grad_key_all[:, :, :half_rows].astype(jnp.bfloat16), "col", -1).astype(
            jnp.float32
        ),
        passed_along(grad_value_all[:, :, :half_rows].astype(jnp.bfloat16), "col", -1).astype(
            jnp.float32
        ),
    )
    grad_key_rot = grad_key_all[:, :, half_rows:] + key_back
    grad_value_heads = grad_value_all[:, :, half_rows:] + value_back
    grad_query_heads, grad_g_query = query_pull(grad_query_rot)
    grad_key_heads, grad_g_key = key_pull(grad_key_rot)

    def heads_last(values):
        return (
            values.astype(jnp.bfloat16)
            .transpose(0, 2, 1, 3)
            .reshape(seq_count, half_rows, query_width)
        )

    grad_qkv = jnp.concatenate(
        [heads_last(grad_query_heads), heads_last(grad_key_heads), heads_last(grad_value_heads)],
        axis=-1,
    )
    query_key_value_gradient = col_gather(grad_qkv)
    reverse_weight = jnp.concatenate(
        [w_query, jnp.tile(w_key, (1, heads_local)), jnp.tile(w_value, (1, heads_local))], axis=1
    )
    grad_w_back = jnp.einsum(
        "pfi,pfj->ij",
        attention_complete,
        query_key_value_gradient,
        preferred_element_type=jnp.float32,
    )
    grad_w_query = grad_w_back[:, :query_width]
    grad_w_key = (
        grad_w_back[:, query_width : 2 * query_width]
        .reshape(feature_share, heads_local, head_size)
        .sum(axis=1)
    )
    grad_w_value = (
        grad_w_back[:, 2 * query_width :].reshape(feature_share, heads_local, head_size).sum(axis=1)
    )
    grad_attn_in = row_sums(
        jnp.einsum(
            "fpy,ty->fpt",
            query_key_value_gradient,
            reverse_weight,
            preferred_element_type=jnp.float32,
        )
    )
    grad_in_norm, grad_g_in = norm_backward(
        inputs_wide, attn_factor, g_in, grad_attn_in, feature_count
    )
    grad_inputs = (grad_middle + grad_in_norm).astype(jnp.bfloat16)
    grad_head_gains = feature_sums(jnp.concatenate([grad_g_query, grad_g_key]))
    shared = lax.psum(
        (
            grad_w_key,
            grad_w_value,
            grad_g_in,
            grad_g_post_attn,
            grad_g_pre_ffn,
            grad_g_post_ffn,
            grad_head_gains,
        ),
        ("dp", "row"),
    )
    grad_w_query, grad_w_out, grad_w_gate, grad_w_up, grad_w_down = (
        lax.psum(grad_w_query.astype(jnp.bfloat16), "dp").astype(jnp.float32),
        lax.psum(grad_w_out.astype(jnp.bfloat16), "dp").astype(jnp.float32),
        lax.psum(grad_w_gate.astype(jnp.bfloat16), "dp").astype(jnp.float32),
        lax.psum(grad_w_up.astype(jnp.bfloat16), "dp").astype(jnp.float32),
        lax.psum(grad_w_down.astype(jnp.bfloat16), "dp").astype(jnp.float32),
    )
    head_gains = shared[6]
    return (
        block_out,
        grad_inputs,
        grad_w_query,
        shared[0],
        shared[1],
        grad_w_out,
        grad_w_gate,
        grad_w_up,
        grad_w_down,
        shared[2],
        head_gains[:head_size],
        head_gains[head_size:],
        shared[3],
        shared[4],
        shared[5],
    )


def solution(mesh):
    placed = (
        P("dp", "row", "col"),
        P("col", "row"),
        P("col", None),
        P("col", None),
        P("row", "col"),
        P("col", "row"),
        P("col", "row"),
        P("row", "col"),
        P("col"),
        P(),
        P(),
        P("col"),
        P("col"),
        P("col"),
        P("dp", "row", "col"),
    )
    return jax.shard_map(
        local,
        mesh=mesh,
        in_specs=placed,
        out_specs=(
            P("dp", "row", "col"),
            P("dp", "row", "col"),
            P("col", "row"),
            P("col", None),
            P("col", None),
            P("row", "col"),
            P("col", "row"),
            P("col", "row"),
            P("row", "col"),
            P("col"),
            P(),
            P(),
            P("col"),
            P("col"),
            P("col"),
        ),
        check_vma=False,
    )
```

profile of v0, /device:TPU:0, one launch (start us, length us, event | category | flops | bytes accessed | tf_op | source)
XLA Modules:
  0.0 1519.2 jit_solution(17066149595980761530)
XLA Ops:
  28.4 10.4 all-to-all-done.1
  43.3 9.9 reduce.37
  60.5 23.6 %all-to-all-done.2 = bf16[2,2,147456]{2,1,0:T(2,128)(2,1)} async-done(((bf16[2,2,147456]{2,1,0:T(2,128)(2,1)}), bf16[2,2,147456]{2,1,0:T(2,128)(2,1)}, u32[]{:S(2)}, u32[]{:S(2)}) %all-to-all-start.2) | async-done | bytes 1179680 | tf_op jit(solution)/shard_map/all_to_all | solution.py:66
  99.7 9.7 collective-permute-done
  110.8 9.6 collective-permute-done.1
  120.9 13.1 all-gather
  139.2 14.0 all_to_all.147
  153.5 6.9 all_to_all.148
  167.9 15.1 all_to_all.150
  185.5 8.1 reshape.1106
  193.6 11.0 reduce.38
  208.0 14.8 all_to_all.151
  236.1 7.8 convolution_bitcast_fusion
  250.2 53.5 %all-gather.12.cloned.1.call-done = bf16[1,1024,1728]{2,1,0:T(8,128)(2,1)} async-done(((bf16[1,512,1728]{2,1,0:T(8,128)(2,1)}), bf16[1,1024,1728]{2,1,0:T(8,128)(2,1)}) %all-gather.12.cloned.1.call-update) | async-done | bytes 3538960 | tf_op jit(solution)/shard_map/all_gather | solution.py:58
  314.7 20.5 %all_to_all.152 = bf16[4,1,256,576]{2,3,1,0:T(8,128)(2,1)S(1)} all-to-all(bf16[4,1,256,576]{2,3,1,0:T(8,128)(2,1)S(1)} %copy.135), channel_id=1, replica_groups=mesh['dp'=16,'row'=4,'col'=2] {'row'}, dimensions={0} | all-to-all | bytes 2359296 | tf_op jit(solution)/shard_map/all_to_all | solution.py:39
  352.3 17.3 %all_to_all.155 = bf16[4,1,256,576]{2,3,1,0:T(8,128)(2,1)} all-to-all(bf16[4,1,256,576]{2,3,1,0:T(8,128)(2,1)S(1)} %broadcast_in_dim.49), channel_id=1, replica_groups=mesh['dp'=16,'row'=4,'col'=2] {'row'}, dimensions={0} | all-to-all | bytes 2359296 | tf_op jit(solution)/shard_map/all_to_all | solution.py:15
  372.0 8.1 reshape.1108
  380.1 11.0 reduce.39
  394.6 16.1 %all_to_all.156 = bf16[2,2,147456]{2,1,0:T(2,128)(2,1)} all-to-all(bf16[2,2,147456]{2,1,0:T(2,128)(2,1)} %reshape.1116), channel_id=1, replica_groups=mesh['dp'=16,'row'=4,'col'=2] {'col'}, dimensions={0} | all-to-all | bytes 2359296 | tf_op jit(solution)/shard_map/all_to_all | solution.py:66
  424.0 9.8 fusion.13
  436.6 91.5 %all-gather.16.cloned.1.call-done = bf16[1,1024,3456]{2,1,0:T(8,128)(2,1)} async-done(((bf16[1,512,3456]{2,1,0:T(8,128)(2,1)}), bf16[1,1024,3456]{2,1,0:T(8,128)(2,1)}) %all-gather.16.cloned.1.call-update) | async-done | bytes 7077904 | tf_op jit(solution)/shard_map/all_gather | solution.py:58
  528.1 9.6 fusion.36
  542.6 20.5 %all_to_all.157 = bf16[4,1,256,576]{2,3,1,0:T(8,128)(2,1)S(1)} all-to-all(bf16[4,1,256,576]{2,3,1,0:T(8,128)(2,1)S(1)} %copy.141), channel_id=1, replica_groups=mesh['dp'=16,'row'=4,'col'=2] {'row'}, dimensions={0} | all-to-all | bytes 2359296 | tf_op jit(solution)/shard_map/all_to_all | solution.py:39
  580.4 15.7 %all_to_all.160 = bf16[4,1,256,576]{2,3,1,0:T(8,128)(2,1)S(1)} all-to-all(bf16[4,1,256,576]{2,3,1,0:T(8,128)(2,1)S(1)} %broadcast_in_dim.52), channel_id=1, replica_groups=mesh['dp'=16,'row'=4,'col'=2] {'row'}, dimensions={0} | all-to-all | bytes 2359296 | tf_op jit(solution)/shard_map/all_to_all | solution.py:15
  597.6 8.1 reshape.1110
  605.7 9.9 reduce.40
  622.6 16.9 %all_gather.30 = bf16[256,1152]{0,1:T(8,128)(2,1)} all-gather(bf16[256,576]{0,1:T(8,128)(2,1)} %param.19), channel_id=1, replica_groups=mesh['dp'=16,'row'=4,'col'=2] {'col'}, dimensions={1}, use_global_device_ids=true | all-gather | bytes 884736 | tf_op jit(solution)/shard_map/all_gather | solution.py:146
  674.7 7.6 fusion.4
  687.7 15.8 %all-gather.18.cloned.1.call-done = bf16[1,1024,768]{2,1,0:T(8,128)(2,1)} async-done(((bf16[1,512,768]{2,1,0:T(8,128)(2,1)}), bf16[1,1024,768]{2,1,0:T(8,128)(2,1)}) %all-gather.18.cloned.1.call-update) | async-done | bytes 1572880 | tf_op jit(solution)/shard_map/all_gather | solution.py:58
  723.2 14.1 all-to-all-done.18
  741.6 329.4 %all-reduce.4 = (f32[576]{0:T(1024)}, f32[512]{0:T(512)S(1)}, f32[576]{0:T(1024)}, f32[576]{0:T(1024)}, f32[576]{0:T(1024)}) all-reduce(f32[576]{0:T(1024)S(1)} %get-tuple-element.29, f32[512]{0:T(512)S(1)} %reduce_sum.362, f32[576]{0:T(1024)S(1)} %get-tuple-element.25, ...), channel_id=1, replica_groups=mesh['dp'=16,'row'=4,'col'=2] {'dp','row'}, use_global_device_ids=true, to_apply=%region_35.36 | all-reduce | flops 2816 | bytes 22528 | tf_op jit(solution)/shard_map/psum | solution.py:339
  1084.7 423.3 %all-reduce.10.cloned.1.call-done = (f32[576,256]{1,0:T(8,128)}, f32[576,256]{1,0:T(8,128)}) async-done(((f32[576,256]{1,0:T(8,128)}, f32[576,256]{1,0:T(8,128)}), (f32[576,256]{1,0:T(8,128)}, f32[576,256]{1,0:T(8,128)})) %all-reduce.10.cloned.1.call-update) | async-done | bytes 1179664 | tf_op jit(solution)/shard_map/psum | solution.py:339
  (272 shorter events, 250.7 us)
Async XLA Ops:
  7.2 11.0 copy-start.38
  7.2 84.5 %all-gather.8.cloned.1.call-start = ((), (), s32[]{:S(2)}) async-start(), calls=%async_computation.21 | async-start | bytes 2654208 | tf_op jit(solution)/shard_map/all_gather | solution.py:144
  19.4 19.4 %all-to-all-start.1 = ((bf16[4,1,256,576]{2,3,1,0:T(8,128)(2,1)}), bf16[4,1,256,576]{2,3,1,0:T(8,128)(2,1)S(1)}, u32[]{:S(2)}, u32[]{:S(2)}) async-start(bf16[4,1,256,576]{2,3,1,0:T(8,128)(2,1)} %broadcast_in_dim.41), calls=%async_computation.1 | async-start | bytes 2359296 | tf_op jit(solution)/shard_map/all_to_all | solution.py:15
  23.7 212.4 %all-gather.10.cloned.1.call-start = ((), (), s32[]{:S(2)}) async-start(), calls=%async_computation.22 | async-start | bytes 11943936 | tf_op jit(solution)/shard_map/all_gather | solution.py:145
  55.6 28.4 %all-to-all-start.2 = ((bf16[2,2,147456]{2,1,0:T(2,128)(2,1)}), bf16[2,2,147456]{2,1,0:T(2,128)(2,1)}, u32[]{:S(2)}, u32[]{:S(2)}) async-start(bf16[2,2,147456]{2,1,0:T(2,128)(2,1)} %reshape.1112), calls=%async_computation.2 | async-start | bytes 2359296 | tf_op jit(solution)/shard_map/all_to_all | solution.py:66
  60.2 243.6 %all-gather.12.cloned.1.call-start = ((), (), s32[]{:S(2)}) async-start(), calls=%async_computation.23 | async-start | bytes 5505024 | tf_op jit(solution)/shard_map/all_gather | solution.py:58
  96.2 14.0 copy-start.25
  96.2 14.0 copy-start.27
  96.3 14.0 copy-start.34
  96.3 13.1 collective-permute-start
  98.3 22.1 %copy-start.29 = (bf16[1,512,256]{2,1,0:T(8,128)(2,1)}, bf16[1,512,256]{2,1,0:T(8,128)(2,1)S(1)}, u32[]{:S(2)}) copy-start(bf16[1,512,256]{2,1,0:T(8,128)(2,1)S(1)} %slice.152) | copy-start | bytes 786436
  98.4 22.1 %collective-permute-start.1 = (bf16[1,512,256]{2,1,0:T(8,128)(2,1)S(1)}, bf16[1,512,256]{2,1,0:T(8,128)(2,1)S(1)}, u32[]{:S(2)}, u32[]{:S(2)}) collective-permute-start(bf16[1,512,256]{2,1,0:T(8,128)(2,1)S(1)} %slice.152), channel_id=1, source_target_pairs={{0,1},{2,3},{4,5},{6,7},{8,9},{10,11},{12,13},{14,15},{16,17},{18,... | collective-permute-start | bytes 786440 | tf_op jit(solution)/shard_map/ppermute | solution.py:46
  110.7 24.1 %copy-start.24 = (bf16[256,576]{0,1:T(8,128)(2,1)S(1)}, bf16[256,576]{0,1:T(8,128)(2,1)}, u32[]{:S(2)}) copy-start(bf16[256,576]{0,1:T(8,128)(2,1)} %param.19) | copy-start | bytes 884740
  120.4 13.6 copy-start.32
  139.2 21.2 %copy-start.37 = (f32[576]{0:T(1024)S(1)}, f32[576]{0:T(1024)}, u32[]{:S(2)}) copy-start(f32[576]{0:T(1024)} %param.26) | copy-start | bytes 6916
  153.2 14.5 copy-start.36
  249.6 174.4 %all-gather.14.cloned.1.call-start = ((), (), s32[]{:S(2)}) async-start(), calls=%async_computation.24 | async-start | bytes 6193152 | tf_op jit(solution)/shard_map/all_gather | solution.py:147
  250.2 277.9 %all-gather.16.cloned.1.call-start = ((), (), s32[]{:S(2)}) async-start(), calls=%async_computation.25 | async-start | bytes 10616832 | tf_op jit(solution)/shard_map/all_gather | solution.py:58
  314.7 27.8 %copy-start.39 = (f32[576]{0:T(1024)S(1)}, f32[576]{0:T(1024)}, u32[]{:S(2)}) copy-start(f32[576]{0:T(1024)} %param.28) | copy-start | bytes 6916
  618.0 21.6 %copy-start.3 = (bf16[4,1,256,576]{2,3,1,0:T(8,128)(2,1)S(1)}, bf16[4,1,256,576]{2,3,1,0:T(8,128)(2,1)}, u32[]{:S(2)}) copy-start(bf16[4,1,256,576]{2,3,1,0:T(8,128)(2,1)} %copy-done.2) | copy-start | bytes 3538948
  618.0 31.6 %all-to-all-start.17 = ((bf16[2,2,147456]{2,1,0:T(2,128)(2,1)}), bf16[2,2,147456]{2,1,0:T(2,128)(2,1)}, u32[]{:S(2)}, u32[]{:S(2)}) async-start(bf16[2,2,147456]{2,1,0:T(2,128)(2,1)} %reshape.1118), calls=%async_computation.17 | async-start | bytes 2359296 | tf_op jit(solution)/shard_map/all_to_all | solution.py:66
  622.6 80.9 %all-gather.18.cloned.1.call-start = ((), (), s32[]{:S(2)}) async-start(), calls=%async_computation.26 | async-start | bytes 2359296 | tf_op jit(solution)/shard_map/all_gather | solution.py:58
  662.1 8.4 collective-permute-start.2
  664.2 9.1 collective-permute-start.3
  674.3 398.1 %all-reduce.12.cloned.1.call-start = ((), (), s32[]{:S(2)}) async-start(), calls=%async_computation.28 | async-start | bytes 13565952 | tf_op jit(solution)/shard_map/psum | solution.py:352
  686.3 17.2 %copy-start.22 = (bf16[72,8,4,256]{3,1,2,0:T(8,128)(2,1)S(1)}, bf16[72,8,4,256]{3,1,2,0:T(8,128)(2,1)}, u32[]{:S(2)}) copy-start(bf16[72,8,4,256]{3,1,2,0:T(8,128)(2,1)} %copy.176) | copy-start | bytes 3538948
  708.6 8.0 all-to-all-start.20
  716.5 20.8 %all-to-all-start.18 = ((bf16[4,1,256,576]{2,3,1,0:T(8,128)(2,1)}), bf16[4,1,256,576]{2,3,1,0:T(8,128)(2,1)S(1)}, u32[]{:S(2)}, u32[]{:S(2)}) async-start(bf16[4,1,256,576]{2,3,1,0:T(8,128)(2,1)} %copy.149), calls=%async_computation.18 | async-start | bytes 2359296 | tf_op jit(solution)/shard_map/all_to_all | solution.py:39
  720.8 16.7 %copy-start.11 = (bf16[1,256,576]{1,2,0:T(8,128)(2,1)S(1)}, bf16[1,256,576]{1,2,0:T(8,128)(2,1)}, u32[]{:S(2)}) copy-start(bf16[1,256,576]{1,2,0:T(8,128)(2,1)} %param.15) | copy-start | bytes 884740
  720.8 787.3 %all-reduce.10.cloned.1.call-start = ((), (), s32[]{:S(2)}) async-start(), calls=%async_computation.27 | async-start | bytes 2359296 | tf_op jit(solution)/shard_map/psum | solution.py:339
  723.2 348.4 %copy-start.13 = (f32[1,256,576]{1,2,0:T(8,128)S(1)}, f32[1,256,576]{1,2,0:T(8,128)}, u32[]{:S(2)}) copy-start(f32[1,256,576]{1,2,0:T(8,128)} %get-tuple-element.43) | copy-start | bytes 1769476
  738.3 333.2 %all-to-all-start.19 = ((f32[2,1,256,1]{2,3,1,0:T(1,128)}), f32[2,1,256,1]{2,3,1,0:T(1,128)S(1)}, u32[]{:S(2)}, u32[]{:S(2)}) async-start(f32[2,1,256,1]{2,3,1,0:T(1,128)} %broadcast_in_dim.55), calls=%async_computation.19 | async-start | bytes 4096 | tf_op jit(solution)/shard_map/all_to_all | solution.py:15
  (31 other events, 84.6 us)
Sparse Core Ops, SparseCore 0:
  11.3 34.4 all-gather.7
  48.0 124.7 all-gather.9
  249.7 54.0 all-gather.11
  305.3 59.6 all-gather.13
  436.7 91.2 all-gather.15
  674.5 28.9 all-gather.17
  708.1 176.5 all-reduce.11
  887.8 620.2 all-reduce.9
where the time goes:
time: 1530 us; the launch traced here: 1520 us
  waiting for transfers between devices  657 us (43%)
  blocking collectives  538 us (35%)
  local copies, waits for them, and re-layouts  138 us (9%)
  other arithmetic  81 us (5%)
  matrix products  59 us (4%)
  starting transfers between devices  30.8 us (2%)
  between operations  15.5 us (1%)
    psum x1, waiting for transfers between devices, local(): lax.psum((grad_w_key, grad_w_value, grad_g_in, grad_g_post_attn, grad_g_p...  423 us
    psum x1, blocking collectives, local(): lax.psum((grad_w_key, grad_w_value, grad_g_in, grad_g_post_attn, grad_g_p...  329 us
    all_gather x3, waiting for transfers between devices, col_gather(): return lax.all_gather(values, 'col', axis=1, tiled=True)  161 us
    all_to_all x10, blocking collectives, sent_to_all(): return lax.all_to_all(copies, axis, split_axis=0, concat_axis=0, tiled=True)  92.5 us
    all_to_all x3, blocking collectives, summed_on_arrival(): lax.all_to_all(cut_along(shard, dim, length), axis, 0, 0, tiled=True)  55.1 us
    unnamed x111, local copies, waits for them, and re-layouts  54.6 us
    unnamed x4, other arithmetic  41.8 us
    another operation x8, local copies, waits for them, and re-layouts, laid_out(): return jnp.moveaxis(parts, 0, dim).reshape(shape)  34.5 us
  transfers between devices with their start and end apart: 18, of which 11 were waited for; matrix products, arithmetic and copies ran while one was open for 12% of the time, Pallas kernels for 0%

commit v1 on v0

--- a/solution.py
+++ b/solution.py
@@ -337,16 +337,19 @@
     grad_inputs = (grad_middle + grad_in_norm).astype(jnp.bfloat16)
     grad_head_gains = feature_sums(jnp.concatenate([grad_g_query, grad_g_key]))
     shared = lax.psum(
-        (
-            grad_w_key,
-            grad_w_value,
-            grad_g_in,
-            grad_g_post_attn,
-            grad_g_pre_ffn,
-            grad_g_post_ffn,
-            grad_head_gains,
+        lax.psum(
+            (
+                grad_w_key,
+                grad_w_value,
+                grad_g_in,
+                grad_g_post_attn,
+                grad_g_pre_ffn,
+                grad_g_post_ffn,
+                grad_head_gains,
+            ),
+            "dp",
         ),
-        ("dp", "row"),
+        "row",
     )
     grad_w_query, grad_w_out, grad_w_gate, grad_w_up, grad_w_down = (
         lax.psum(grad_w_query.astype(jnp.bfloat16), "dp").astype(jnp.float32),

time: 1530 us -> 1100 us (0.72)
  blocking collectives: 538 us -> 297 us
  waiting for transfers between devices: 657 us -> 461 us
    psum x1, waiting for transfers between devices: 423 us -> 115 us  [local(): lax.psum((grad_w_key, grad_w_value, grad_g_in, grad_g_post_attn, grad_g_p...]
    psum x1, blocking collectives: 329 us -> 70.8 us  [local(): lax.psum((grad_w_key, grad_w_value, grad_g_in, grad_g_post_attn, grad_g_p...]
    psum x1, waiting for transfers between devices: 0.01 us -> 86.7 us  [local(): lax.psum(grad_w_query.astype(jnp.bfloat16), 'dp').astype(jnp.float32)]
    psum x0 -> x1, waiting for transfers between devices: none -> 37.1 us  [local(): lax.psum(lax.psum((grad_w_key, grad_w_value, grad_g_in, grad_g_post_attn,...]
    psum x0 -> x1, blocking collectives: none -> 17.5 us  [local(): lax.psum(lax.psum((grad_w_key, grad_w_value, grad_g_in, grad_g_post_attn,...]
    unnamed x111 -> x137, local copies, waits for them, and re-layouts: 54.6 us -> 57.1 us
  transfers between devices with their start and end apart: 18 -> 19, of which waited for: 11 -> 12; matrix products, arithmetic and copies ran while one was open for 12% -> 17% of each run, Pallas kernels for 0% -> 0%
where the time goes in v1:
time: 1100 us; the launch traced here: 1090 us
  waiting for transfers between devices  461 us (42%)
  blocking collectives  297 us (27%)
  local copies, waits for them, and re-layouts  141 us (13%)
  other arithmetic  85.2 us (8%)
  matrix products  59.6 us (5%)
  starting transfers between devices  31 us (3%)
  between operations  15.3 us (1%)
    all_gather x3, waiting for transfers between devices, col_gather(): return lax.all_gather(values, 'col', axis=1, tiled=True)  163 us
    psum x1, waiting for transfers between devices, local(): lax.psum((grad_w_key, grad_w_value, grad_g_in, grad_g_post_attn, grad_g_p...  115 us
    all_to_all x10, blocking collectives, sent_to_all(): return lax.all_to_all(copies, axis, split_axis=0, concat_axis=0, tiled=True)  92.7 us
    psum x1, waiting for transfers between devices, local(): lax.psum(grad_w_query.astype(jnp.bfloat16), 'dp').astype(jnp.float32)  86.7 us
    psum x1, blocking collectives, local(): lax.psum((grad_w_key, grad_w_value, grad_g_in, grad_g_post_attn, grad_g_p...  70.8 us
    unnamed x137, local copies, waits for them, and re-layouts  57.1 us
    all_to_all x3, blocking collectives, summed_on_arrival(): lax.all_to_all(cut_along(shard, dim, length), axis, 0, 0, tiled=True)  55.1 us
    unnamed x4, other arithmetic  43 us
  transfers between devices with their start and end apart: 19, of which 12 were waited for; matrix products, arithmetic and copies ran while one was open for 17% of the time, Pallas kernels for 0%

profile of v1, /device:TPU:0, one launch (start us, length us, event | category | flops | bytes accessed | tf_op | source)
XLA Modules:
  0.0 1090.2 jit_solution(17234515800421923910)
XLA Ops:
  29.0 10.3 all-to-all-done.1
  43.9 9.9 reduce.37
  61.1 24.3 %all-to-all-done.2 = bf16[2,2,147456]{2,1,0:T(2,128)(2,1)} async-done(((bf16[2,2,147456]{2,1,0:T(2,128)(2,1)}), bf16[2,2,147456]{2,1,0:T(2,128)(2,1)}, u32[]{:S(2)}, u32[]{:S(2)}) %all-to-all-start.2) | async-done | bytes 1179680 | tf_op jit(solution)/shard_map/all_to_all | solution.py:66
  101.7 9.7 collective-permute-done
  112.8 9.6 collective-permute-done.1
  122.9 13.1 %all-gather = bf16[1024,256]{1,0:T(8,128)(2,1)S(1)} all-gather(bf16[512,256]{1,0:T(8,128)(2,1)S(1)} %convolution_convert_fusion.3), channel_id=2, replica_groups=mesh['dp'=16,'row'=4,'col'=2] {'col'}, dimensions={0}, use_global_device_ids=true | all-gather | bytes 786432 | tf_op jit(solution)/shard_map/all_gather | solution.py:58
  141.2 14.0 %all_to_all.147 = bf16[4,1,256,576]{2,3,1,0:T(8,128)(2,1)S(1)} all-to-all(bf16[4,1,256,576]{2,3,1,0:T(8,128)(2,1)S(1)} %copy.130), channel_id=1, replica_groups=mesh['dp'=16,'row'=4,'col'=2] {'row'}, dimensions={0} | all-to-all | bytes 2359296 | tf_op jit(solution)/shard_map/all_to_all | solution.py:39
  170.0 15.1 %all_to_all.150 = bf16[4,1,256,576]{2,3,1,0:T(8,128)(2,1)} all-to-all(bf16[4,1,256,576]{2,3,1,0:T(8,128)(2,1)S(1)} %broadcast_in_dim.46), channel_id=1, replica_groups=mesh['dp'=16,'row'=4,'col'=2] {'row'}, dimensions={0} | all-to-all | bytes 2359296 | tf_op jit(solution)/shard_map/all_to_all | solution.py:15
  187.6 8.1 reshape.1106
  195.7 11.1 %reduce.38 = bf16[1024,576]{1,0:T(8,128)(2,1)} reduce(bf16[1024,1,576]{2,1,0:T(2,128)(2,1)} %bitcast.255, bf16[]{:T(256)} %broadcast.838), dimensions={1}, to_apply=%bitcast.218.reduce_sub_computation | reduce | bytes 2359298
  210.2 14.7 %all_to_all.151 = bf16[2,2,147456]{2,1,0:T(2,128)(2,1)} all-to-all(bf16[2,2,147456]{2,1,0:T(2,128)(2,1)} %reshape.1114), channel_id=1, replica_groups=mesh['dp'=16,'row'=4,'col'=2] {'col'}, dimensions={0} | all-to-all | bytes 2359296 | tf_op jit(solution)/shard_map/all_to_all | solution.py:66
  238.5 7.8 convolution_bitcast_fusion
  252.6 53.4 %all-gather.12.cloned.1.call-done = bf16[1,1024,1728]{2,1,0:T(8,128)(2,1)} async-done(((bf16[1,512,1728]{2,1,0:T(8,128)(2,1)}), bf16[1,1024,1728]{2,1,0:T(8,128)(2,1)}) %all-gather.12.cloned.1.call-update) | async-done | bytes 3538960 | tf_op jit(solution)/shard_map/all_gather | solution.py:58
  316.9 20.5 %all_to_all.152 = bf16[4,1,256,576]{2,3,1,0:T(8,128)(2,1)S(1)} all-to-all(bf16[4,1,256,576]{2,3,1,0:T(8,128)(2,1)S(1)} %copy.135), channel_id=1, replica_groups=mesh['dp'=16,'row'=4,'col'=2] {'row'}, dimensions={0} | all-to-all | bytes 2359296 | tf_op jit(solution)/shard_map/all_to_all | solution.py:39
  355.1 17.5 %all_to_all.155 = bf16[4,1,256,576]{2,3,1,0:T(8,128)(2,1)} all-to-all(bf16[4,1,256,576]{2,3,1,0:T(8,128)(2,1)S(1)} %broadcast_in_dim.49), channel_id=1, replica_groups=mesh['dp'=16,'row'=4,'col'=2] {'row'}, dimensions={0} | all-to-all | bytes 2359296 | tf_op jit(solution)/shard_map/all_to_all | solution.py:15
  375.0 8.1 reshape.1108
  383.1 11.0 %reduce.39 = bf16[1024,576]{1,0:T(8,128)(2,1)} reduce(bf16[1024,1,576]{2,1,0:T(2,128)(2,1)} %bitcast.257, bf16[]{:T(256)} %broadcast.838), dimensions={1}, to_apply=%bitcast.220.reduce_sub_computation | reduce | bytes 2359298
  397.6 16.3 %all_to_all.156 = bf16[2,2,147456]{2,1,0:T(2,128)(2,1)} all-to-all(bf16[2,2,147456]{2,1,0:T(2,128)(2,1)} %reshape.1116), channel_id=1, replica_groups=mesh['dp'=16,'row'=4,'col'=2] {'col'}, dimensions={0} | all-to-all | bytes 2359296 | tf_op jit(solution)/shard_map/all_to_all | solution.py:66
  427.3 9.8 fusion.13
  439.9 91.2 %all-gather.16.cloned.1.call-done = bf16[1,1024,3456]{2,1,0:T(8,128)(2,1)} async-done(((bf16[1,512,3456]{2,1,0:T(8,128)(2,1)}), bf16[1,1024,3456]{2,1,0:T(8,128)(2,1)}) %all-gather.16.cloned.1.call-update) | async-done | bytes 7077904 | tf_op jit(solution)/shard_map/all_gather | solution.py:58
  531.1 9.6 fusion.36
  545.6 20.5 %all_to_all.157 = bf16[4,1,256,576]{2,3,1,0:T(8,128)(2,1)S(1)} all-to-all(bf16[4,1,256,576]{2,3,1,0:T(8,128)(2,1)S(1)} %copy.141), channel_id=1, replica_groups=mesh['dp'=16,'row'=4,'col'=2] {'row'}, dimensions={0} | all-to-all | bytes 2359296 | tf_op jit(solution)/shard_map/all_to_all | solution.py:39
  584.5 15.7 %all_to_all.160 = bf16[4,1,256,576]{2,3,1,0:T(8,128)(2,1)S(1)} all-to-all(bf16[4,1,256,576]{2,3,1,0:T(8,128)(2,1)S(1)} %broadcast_in_dim.52), channel_id=1, replica_groups=mesh['dp'=16,'row'=4,'col'=2] {'row'}, dimensions={0} | all-to-all | bytes 2359296 | tf_op jit(solution)/shard_map/all_to_all | solution.py:15
  601.7 8.1 reshape.1110
  609.8 11.0 %reduce.40 = bf16[1024,576]{1,0:T(8,128)(2,1)} reduce(bf16[1024,1,576]{2,1,0:T(2,128)(2,1)} %bitcast.253, bf16[]{:T(256)} %broadcast.838), dimensions={1}, to_apply=%bitcast.222.reduce_sub_computation | reduce | bytes 2359298
  628.8 16.9 %all_gather.30 = bf16[256,1152]{0,1:T(8,128)(2,1)} all-gather(bf16[256,576]{0,1:T(8,128)(2,1)} %param.19), channel_id=1, replica_groups=mesh['dp'=16,'row'=4,'col'=2] {'col'}, dimensions={1}, use_global_device_ids=true | all-gather | bytes 884736 | tf_op jit(solution)/shard_map/all_gather | solution.py:146
  683.5 18.8 %all-gather.18.cloned.1.call-done = bf16[1,1024,768]{2,1,0:T(8,128)(2,1)} async-done(((bf16[1,512,768]{2,1,0:T(8,128)(2,1)}), bf16[1,1024,768]{2,1,0:T(8,128)(2,1)}) %all-gather.18.cloned.1.call-update) | async-done | bytes 1572880 | tf_op jit(solution)/shard_map/all_gather | solution.py:58
  734.2 114.9 %all-reduce.13.cloned.1.call-done = (f32[576,256]{1,0:T(8,128)}, f32[576,256]{1,0:T(8,128)}) async-done(((f32[576,256]{1,0:T(8,128)}, f32[576,256]{1,0:T(8,128)}), (f32[576,256]{1,0:T(8,128)}, f32[576,256]{1,0:T(8,128)})) %all-reduce.13.cloned.1.call-update) | async-done | bytes 1179664 | tf_op jit(solution)/shard_map/psum | solution.py:340
  853.5 70.8 %all-reduce.4 = (f32[576]{0:T(1024)S(1)}, f32[512]{0:T(512)S(1)}, f32[576]{0:T(1024)S(1)}, f32[576]{0:T(1024)S(1)}, f32[576]{0:T(1024)S(1)}) all-reduce(f32[576]{0:T(1024)S(1)} %get-tuple-element.29, f32[512]{0:T(512)S(1)} %reduce_sum.362, f32[576]{0:T(1024)S(1)} %copy-done.45, ...), channel_id=1, replica_groups=mesh['dp'=16,'row'=4,'col'=2] {'dp'}, use_global_device_ids=true, to_apply=%region_37.38 | all-reduce | flops 2816 | bytes 22528 | tf_op jit(solution)/shard_map/psum | solution.py:340
  924.3 17.5 %all-reduce.6 = (f32[576]{0:T(1024)}, f32[512]{0:T(512)S(1)}, f32[576]{0:T(1024)}, f32[576]{0:T(1024)}, f32[576]{0:T(1024)}) all-reduce(f32[576]{0:T(1024)S(1)} %get-tuple-element.31, f32[512]{0:T(512)S(1)} %get-tuple-element.32, f32[576]{0:T(1024)S(1)} %get-tuple-element.33, ...), channel_id=1, replica_groups=mesh['dp'=16,'row'=4,'col'=2] {'row'}, use_global_device_ids=true, to_apply=%region_38.39 | all-reduce | flops 2816 | bytes 22528 | tf_op jit(solution)/shard_map/psum | solution.py:339
  943.3 86.7 %all-reduce.17.cloned.1.call-done = (bf16[576,256]{1,0:T(8,128)(2,1)}, bf16[256,576]{0,1:T(8,128)(2,1)}, bf16[576,1728]{1,0:T(8,128)(2,1)}, bf16[576,1728]{1,0:T(8,128)(2,1)}, bf16[1728,576]{0,1:T(8,128)(2,1)}) async-done(((bf16[576,256]{1,0:T(8,128)(2,1)}, bf16[256,576]{0,1:T(8,128)(2,1)}, bf16[576,1728]{1,0:T(8,128)(2,1)}, bf16[576,1728]{1,0:T(8,128)(2,1)}, bf16[1728,576]{0,1:T(8,128)(2,1)}), ...) | async-done | bytes 6561808 | tf_op jit(solution)/shard_map/psum | solution.py:355
  1042.3 37.1 %all-reduce.15.cloned.1.call-done = (f32[576,256]{1,0:T(8,128)}, f32[576,256]{1,0:T(8,128)}) async-done(((f32[576,256]{1,0:T(8,128)}, f32[576,256]{1,0:T(8,128)}), (f32[576,256]{1,0:T(8,128)}, f32[576,256]{1,0:T(8,128)})) %all-reduce.15.cloned.1.call-update) | async-done | bytes 1179664 | tf_op jit(solution)/shard_map/psum | solution.py:339
  (302 shorter events, 271.4 us)
Async XLA Ops:
  7.2 85.9 %all-gather.8.cloned.1.call-start = ((), (), s32[]{:S(2)}) async-start(), calls=%async_computation.21 | async-start | bytes 2654208 | tf_op jit(solution)/shard_map/all_gather | solution.py:144
  20.0 19.4 %all-to-all-start.1 = ((bf16[4,1,256,576]{2,3,1,0:T(8,128)(2,1)}), bf16[4,1,256,576]{2,3,1,0:T(8,128)(2,1)S(1)}, u32[]{:S(2)}, u32[]{:S(2)}) async-start(bf16[4,1,256,576]{2,3,1,0:T(8,128)(2,1)} %broadcast_in_dim.41), calls=%async_computation.1 | async-start | bytes 2359296 | tf_op jit(solution)/shard_map/all_to_all | solution.py:15
  24.3 214.2 %all-gather.10.cloned.1.call-start = ((), (), s32[]{:S(2)}) async-start(), calls=%async_computation.22 | async-start | bytes 11943936 | tf_op jit(solution)/shard_map/all_gather | solution.py:145
  56.2 29.2 %all-to-all-start.2 = ((bf16[2,2,147456]{2,1,0:T(2,128)(2,1)}), bf16[2,2,147456]{2,1,0:T(2,128)(2,1)}, u32[]{:S(2)}, u32[]{:S(2)}) async-start(bf16[2,2,147456]{2,1,0:T(2,128)(2,1)} %reshape.1112), calls=%async_computation.2 | async-start | bytes 2359296 | tf_op jit(solution)/shard_map/all_to_all | solution.py:66
  60.8 245.2 %all-gather.12.cloned.1.call-start = ((), (), s32[]{:S(2)}) async-start(), calls=%async_computation.23 | async-start | bytes 5505024 | tf_op jit(solution)/shard_map/all_gather | solution.py:58
  61.0 36.0 %copy-start.53 = (f32[128]{0:T(128)}, f32[128]{0:T(128)S(1)}, u32[]{:S(2)}) copy-start(f32[128]{0:T(128)S(1)} %negate_power_fusion) | copy-start | bytes 1540
  61.1 36.0 %copy-start.38 = (f32[512]{0:T(512)}, f32[512]{0:T(512)S(1)}, u32[]{:S(2)}) copy-start(f32[512]{0:T(512)S(1)} %fusion.121) | copy-start | bytes 6148
  98.4 13.0 %collective-permute-start = (bf16[1,512,256]{2,1,0:T(8,128)(2,1)S(1)}, bf16[1,512,256]{2,1,0:T(8,128)(2,1)S(1)}, u32[]{:S(2)}, u32[]{:S(2)}) collective-permute-start(bf16[1,512,256]{2,1,0:T(8,128)(2,1)S(1)} %maximum_bitcast_fusion.6), channel_id=1, source_target_pairs={{0,1},{2,3},{4,5},{6,7},{8,9},{10,11},{12,13},{14,15},{16,17},{18,... | collective-permute-start | bytes 786440 | tf_op jit(solution)/shard_map/ppermute | solution.py:46
  100.4 22.1 %copy-start.24 = (bf16[1,512,256]{2,1,0:T(8,128)(2,1)}, bf16[1,512,256]{2,1,0:T(8,128)(2,1)S(1)}, u32[]{:S(2)}) copy-start(bf16[1,512,256]{2,1,0:T(8,128)(2,1)S(1)} %slice.152) | copy-start | bytes 786436
  100.4 22.1 %collective-permute-start.1 = (bf16[1,512,256]{2,1,0:T(8,128)(2,1)S(1)}, bf16[1,512,256]{2,1,0:T(8,128)(2,1)S(1)}, u32[]{:S(2)}, u32[]{:S(2)}) collective-permute-start(bf16[1,512,256]{2,1,0:T(8,128)(2,1)S(1)} %slice.152), channel_id=1, source_target_pairs={{0,1},{2,3},{4,5},{6,7},{8,9},{10,11},{12,13},{14,15},{16,17},{18,... | collective-permute-start | bytes 786440 | tf_op jit(solution)/shard_map/ppermute | solution.py:46
  112.8 24.0 %copy-start.19 = (bf16[256,576]{0,1:T(8,128)(2,1)S(1)}, bf16[256,576]{0,1:T(8,128)(2,1)}, u32[]{:S(2)}) copy-start(bf16[256,576]{0,1:T(8,128)(2,1)} %param.19) | copy-start | bytes 884740
  141.2 21.2 %copy-start.32 = (f32[576]{0:T(1024)S(1)}, f32[576]{0:T(1024)}, u32[]{:S(2)}) copy-start(f32[576]{0:T(1024)} %param.26) | copy-start | bytes 6916
  251.9 175.4 %all-gather.14.cloned.1.call-start = ((), (), s32[]{:S(2)}) async-start(), calls=%async_computation.24 | async-start | bytes 6193152 | tf_op jit(solution)/shard_map/all_gather | solution.py:147
  252.5 278.5 %all-gather.16.cloned.1.call-start = ((), (), s32[]{:S(2)}) async-start(), calls=%async_computation.25 | async-start | bytes 10616832 | tf_op jit(solution)/shard_map/all_gather | solution.py:58
  316.9 27.8 %copy-start.40 = (f32[576]{0:T(1024)S(1)}, f32[576]{0:T(1024)}, u32[]{:S(2)}) copy-start(f32[576]{0:T(1024)} %param.28) | copy-start | bytes 6916
  624.3 21.4 %all-to-all-start.17 = ((bf16[2,2,147456]{2,1,0:T(2,128)(2,1)}), bf16[2,2,147456]{2,1,0:T(2,128)(2,1)}, u32[]{:S(2)}, u32[]{:S(2)}) async-start(bf16[2,2,147456]{2,1,0:T(2,128)(2,1)} %reshape.1118), calls=%async_computation.17 | async-start | bytes 2359296 | tf_op jit(solution)/shard_map/all_to_all | solution.py:66
  628.7 73.6 %all-gather.18.cloned.1.call-start = ((), (), s32[]{:S(2)}) async-start(), calls=%async_computation.26 | async-start | bytes 2359296 | tf_op jit(solution)/shard_map/all_gather | solution.py:58
  660.9 8.4 collective-permute-start.2
  663.0 9.1 collective-permute-start.3
  673.2 175.9 %all-reduce.13.cloned.1.call-start = ((), (), s32[]{:S(2)}) async-start(), calls=%async_computation.27 | async-start | bytes 2359296 | tf_op jit(solution)/shard_map/psum | solution.py:340
  706.2 323.8 %all-reduce.17.cloned.1.call-start = ((), (), s32[]{:S(2)}) async-start(), calls=%async_computation.29 | async-start | bytes 13565952 | tf_op jit(solution)/shard_map/psum | solution.py:355
  721.6 8.2 all-to-all-start.20
  729.7 119.6 %copy-start.9 = (bf16[1,256,576]{1,2,0:T(8,128)(2,1)S(1)}, bf16[1,256,576]{1,2,0:T(8,128)(2,1)}, u32[]{:S(2)}) copy-start(bf16[1,256,576]{1,2,0:T(8,128)(2,1)} %param.15) | copy-start | bytes 884740
  729.7 119.6 %copy-start.42 = (f32[256]{0:T(256)S(1)}, f32[256]{0:T(256)}, u32[]{:S(2)}) copy-start(f32[256]{0:T(256)} %copy-done.41) | copy-start | bytes 3076
  729.7 119.4 %all-to-all-start.18 = ((bf16[4,1,256,576]{2,3,1,0:T(8,128)(2,1)}), bf16[4,1,256,576]{2,3,1,0:T(8,128)(2,1)S(1)}, u32[]{:S(2)}, u32[]{:S(2)}) async-start(bf16[4,1,256,576]{2,3,1,0:T(8,128)(2,1)} %copy.149), calls=%async_computation.18 | async-start | bytes 2359296 | tf_op jit(solution)/shard_map/all_to_all | solution.py:39
  734.1 119.3 %copy-start.43 = (f32[576]{0:T(1024)S(1)}, f32[576]{0:T(1024)}, u32[]{:S(2)}) copy-start(f32[576]{0:T(1024)} %get-tuple-element.27) | copy-start | bytes 6916
  734.1 119.4 %copy-start.44 = (f32[576]{0:T(1024)S(1)}, f32[576]{0:T(1024)}, u32[]{:S(2)}) copy-start(f32[576]{0:T(1024)} %get-tuple-element.23) | copy-start | bytes 6916
  734.1 119.4 %copy-start.45 = (f32[576]{0:T(1024)S(1)}, f32[576]{0:T(1024)}, u32[]{:S(2)}) copy-start(f32[576]{0:T(1024)} %get-tuple-element.25) | copy-start | bytes 6916
  734.1 208.3 %copy-start.11 = (f32[1,256,576]{1,2,0:T(8,128)S(1)}, f32[1,256,576]{1,2,0:T(8,128)}, u32[]{:S(2)}) copy-start(f32[1,256,576]{1,2,0:T(8,128)} %get-tuple-element.50) | copy-start | bytes 1769476
  734.1 208.3 %copy-start.50 = (f32[256]{0:T(256)S(1)}, f32[256]{0:T(256)}, u32[]{:S(2)}) copy-start(f32[256]{0:T(256)} %get-tuple-element.79) | copy-start | bytes 3076
  734.1 345.3 %all-reduce.15.cloned.1.call-start = ((), (), s32[]{:S(2)}) async-start(), calls=%async_computation.28 | async-start | bytes 2359296 | tf_op jit(solution)/shard_map/psum | solution.py:339
  850.2 92.2 %all-to-all-start.19 = ((f32[2,1,256,1]{2,3,1,0:T(1,128)}), f32[2,1,256,1]{2,3,1,0:T(1,128)S(1)}, u32[]{:S(2)}, u32[]{:S(2)}) async-start(f32[2,1,256,1]{2,3,1,0:T(1,128)} %broadcast_in_dim.55), calls=%async_computation.19 | async-start | bytes 4096 | tf_op jit(solution)/shard_map/all_to_all | solution.py:15
  (45 other events, 190.0 us)
Sparse Core Ops, SparseCore 0:
  11.3 34.4 all-gather.7
  48.1 125.3 all-gather.9
  252.1 53.8 all-gather.11
  307.5 59.6 all-gather.13
  440.0 90.9 all-gather.15
  673.3 28.9 all-gather.17
  706.4 142.6 all-reduce.12
  853.1 176.8 all-reduce.16
  1032.4 46.9 all-reduce.14
